TPU v7x, 32 devices: a whole 2x2x4 slice. The times are simulated.
32 devices in a mesh: space: 8 (over z, x), var: 4 (over y, core).
Axes of the slice: x: 2, y: 2, z: 4, core: 2. Of those that a mesh axis runs over, the one named last changes fastest.
Arguments:
- tensor_field: bfloat16 [128, 262144], P('var', 'space'), may hold values from -32 to 32
- start_basis: float32 [128, 32], replicated, may hold values from -5 to 5
Outputs:
- leading_basis: float32 [128, 32], replicated
- core_tensor: float32 [32, 262144], P(None, ('space', 'var'))
All inputs are finite; a program needn't handle non-finite values.
Results may differ from a plain program's by a relative error of at most 0.0024.
Values may be sent and summed in bfloat16 or wider, within the bound.
A program may use at most 64 MiB of HBM per device.

v0:
```python
import jax
import jax.numpy as jnp
from jax import lax
from jax.sharding import PartitionSpec as P

ITERS = 8


def solve_rows(factor, product):
    return lax.linalg.triangular_solve(factor, product.T, left_side=True, lower=True).T


def per_device(tensor_field, start_basis):
    fibres = lax.all_to_all(tensor_field, "var", split_axis=1, concat_axis=0, tiled=True)
    partial_gram = jnp.einsum("vc,wc->vw", fibres, fibres, preferred_element_type=jnp.float32)
    leading_basis = start_basis
    gram_matrix = lax.psum(partial_gram, ("space", "var"))
    for iteration in range(ITERS):
        product = jnp.dot(
            gram_matrix,
            leading_basis,
            precision=lax.Precision.HIGHEST,
            preferred_element_type=jnp.float32,
        )
        cross_gram = jnp.dot(
            product.T, product, precision=lax.Precision.HIGHEST, preferred_element_type=jnp.float32
        )
        factor = jnp.linalg.cholesky(cross_gram)
        leading_basis = solve_rows(factor, product)
    narrow = leading_basis.astype(jnp.bfloat16)
    slice_rows = tensor_field.shape[0]
    own_rows = lax.dynamic_slice_in_dim(narrow, lax.axis_index("var") * slice_rows, slice_rows, 0)
    core_term = jnp.einsum("vr,vc->rc", own_rows, tensor_field, preferred_element_type=jnp.float32)
    core_tensor = lax.psum_scatter(core_term, "var", scatter_dimension=1, tiled=True)
    return (leading_basis, core_tensor)


def solution(mesh):
    return jax.shard_map(
        per_device,
        mesh=mesh,
        in_specs=(P("var", "space"), P()),
        out_specs=(P(), P(None, ("space", "var"))),
        check_vma=False,
    )
```

profile of v0, /device:TPU:0, one launch (start us, length us, event | category | flops | bytes accessed | tf_op | source)
XLA Modules:
  0.0 278.2 jit_solution(11987983422395595650)
XLA Ops:
  7.2 1.7 copy.40
  9.0 29.7 %all_to_all.19 = bf16[32,4,8192]{2,0,1:T(8,128)(2,1)S(1)} all-to-all(bf16[32,4,8192]{2,0,1:T(8,128)(2,1)S(1)} %bitcast.142), channel_id=1, replica_groups=mesh['space'=8,'var'=4] {'var'}, dimensions={1} | all-to-all | bytes 4194304 | tf_op jit(solution)/shard_map/all_to_all | solution.py:14
  38.7 1.3 fusion.55
  40.1 117.9 %all-reduce.2.cloned.1.call-done = f32[128,128]{1,0:T(8,128)} async-done(((f32[128,128]{1,0:T(8,128)}), f32[128,128]{1,0:T(8,128)}) %all-reduce.2.cloned.1.call-update) | async-done | bytes 65552 | tf_op jit(solution)/shard_map/psum | solution.py:17
  158.1 1.1 fusion.56
  159.4 2.9 %cholesky.134 = f32[32,32]{1,0:T(8,128)S(1)} custom-call(f32[32,32]{1,0:T(8,128)S(1)} %fusion.38), custom_call_target="Cholesky" | custom-call | tf_op jit(solution)/shard_map/jit(cholesky)/cholesky | solution.py:28
  163.7 2.4 custom-call.12
  167.7 2.9 %cholesky.145 = f32[32,32]{1,0:T(8,128)S(1)} custom-call(f32[32,32]{1,0:T(8,128)S(1)} %fusion.34), custom_call_target="Cholesky" | custom-call | tf_op jit(solution)/shard_map/jit(cholesky)/cholesky | solution.py:28
  171.9 2.4 custom-call.13
  175.9 2.9 %cholesky.156 = f32[32,32]{1,0:T(8,128)S(1)} custom-call(f32[32,32]{1,0:T(8,128)S(1)} %fusion.30), custom_call_target="Cholesky" | custom-call | tf_op jit(solution)/shard_map/jit(cholesky)/cholesky | solution.py:28
  180.2 2.4 custom-call.14
  184.1 2.9 %cholesky.167 = f32[32,32]{1,0:T(8,128)S(1)} custom-call(f32[32,32]{1,0:T(8,128)S(1)} %fusion.26), custom_call_target="Cholesky" | custom-call | tf_op jit(solution)/shard_map/jit(cholesky)/cholesky | solution.py:28
  188.4 2.4 custom-call.15
  192.4 2.9 %cholesky.178 = f32[32,32]{1,0:T(8,128)S(1)} custom-call(f32[32,32]{1,0:T(8,128)S(1)} %fusion.22), custom_call_target="Cholesky" | custom-call | tf_op jit(solution)/shard_map/jit(cholesky)/cholesky | solution.py:28
  196.6 2.4 custom-call.16
  199.3 1.0 fusion.66
  200.6 2.9 %cholesky.189 = f32[32,32]{1,0:T(8,128)S(1)} custom-call(f32[32,32]{1,0:T(8,128)S(1)} %fusion.18), custom_call_target="Cholesky" | custom-call | tf_op jit(solution)/shard_map/jit(cholesky)/cholesky | solution.py:28
  204.9 2.4 custom-call.17
  208.9 2.9 %cholesky.200 = f32[32,32]{1,0:T(8,128)S(1)} custom-call(f32[32,32]{1,0:T(8,128)S(1)} %fusion.14), custom_call_target="Cholesky" | custom-call | tf_op jit(solution)/shard_map/jit(cholesky)/cholesky | solution.py:28
  213.1 2.4 custom-call.18
  216.3 2.9 %cholesky.211 = f32[32,32]{1,0:T(8,128)S(1)} custom-call(f32[32,32]{1,0:T(8,128)S(1)} %fusion.10), custom_call_target="Cholesky" | custom-call | tf_op jit(solution)/shard_map/jit(cholesky)/cholesky | solution.py:28
  220.5 2.4 custom-call.19
  223.2 2.7 fusion.53
  225.9 45.4 %reduce-scatter.2.cloned.1.call-done = f32[32,8192]{1,0:T(8,128)} async-done(((f32[32,32768]{1,0:T(8,128)}), f32[32,8192]{1,0:T(8,128)}) %reduce-scatter.2.cloned.1.call-update) | async-done | bytes 1048592 | tf_op jit(solution)/shard_map/reduce_scatter | solution.py:34
  (74 shorter events, 19.9 us)
Async XLA Ops:
  7.2 150.9 %copy-start = (f32[128,32]{0,1:T(8,128)S(1)}, f32[128,32]{0,1:T(8,128)}, u32[]{:S(2)}) copy-start(f32[128,32]{0,1:T(8,128)} %param.6) | copy-start | bytes 49156
  7.2 150.9 %all-reduce.2.cloned.1.call-start = ((), (), s32[]{:S(2)}) async-start(), calls=%async_computation.2 | async-start | bytes 131072 | tf_op jit(solution)/shard_map/psum | solution.py:17
  40.0 183.2 %copy-start.1 = (bf16[32,32768]{1,0:T(8,128)(2,1)S(1)}, bf16[32,32768]{1,0:T(8,128)(2,1)}, u32[]{:S(2)}) copy-start(bf16[32,32768]{1,0:T(8,128)(2,1)} %param.5) | copy-start | bytes 6291460
  40.1 231.3 %reduce-scatter.2.cloned.1.call-start = ((), (), s32[]{:S(2)}) async-start(), calls=%async_computation.3 | async-start | bytes 5242880 | tf_op jit(solution)/shard_map/reduce_scatter | solution.py:34
  158.1 57.7 %copy-start.2 = (f32[128,128]{1,0:T(8,128)S(1)}, f32[128,128]{1,0:T(8,128)}, u32[]{:S(2)}) copy-start(f32[128,128]{1,0:T(8,128)} %all-reduce.2.cloned.1.call-done) | copy-start | bytes 196612
  223.2 2.7 copy-start.3
Sparse Core Ops, SparseCore 0:
  40.2 117.8 all-reduce.1
  226.1 45.2 reduce-scatter.1
where the time goes:
time: 279 us; the launch traced here: 278 us
  waiting for transfers between devices  163 us (58%)
  other arithmetic  53.6 us (19%)
  blocking collectives  29.7 us (11%)
  matrix products  14.7 us (5%)
  between operations  14.4 us (5%)
    psum x1, waiting for transfers between devices, per_device(): gram_matrix = lax.psum(partial_gram, ('space', 'var'))  118 us
    reduce_scatter x1, waiting for transfers between devices, per_device(): lax.psum_scatter(core_term, 'var', scatter_dimension=1, tiled=True)  45.4 us
    all_to_all x1, blocking collectives, per_device(): lax.all_to_all(tensor_field, 'var', split_axis=1, concat_axis=0, tiled=True)  29.7 us
    another operation x24, other arithmetic, per_device(): factor = jnp.linalg.cholesky(cross_gram)  28.8 us
    another operation x16, other arithmetic, solve_rows(): lax.linalg.triangular_solve(factor, product.T, left_side=True, lower=True)  24.7 us
    dot_general x8, matrix products, per_device(): jnp.dot(gram_matrix, leading_basis, precision=lax.Precision.HIGHEST, pref...  7.49 us
  transfers between devices with their start and end apart: 2, of which 2 were waited for; matrix products, arithmetic and copies ran while one was open for 0% of the time, Pallas kernels for 0%

commit v1 on v0

v1 whole, which is shorter than its diff:
```python
import jax
import jax.numpy as jnp
from jax import lax
from jax.experimental import pallas as pl
from jax.experimental.pallas import tpu as pltpu
from jax.sharding import PartitionSpec as P

ITERS = 8
SUB = 8


def eliminate(cross_gram, rows):
    rank, width = rows.shape
    blocks = rank // SUB
    rows = [rows[b * SUB : (b + 1) * SUB] for b in range(blocks)]
    columns = [
        [
            jnp.broadcast_to(cross_gram[b * SUB : (b + 1) * SUB, k : k + 1], (SUB, width))
            if b >= k // SUB
            else None
            for b in range(blocks)
        ]
        for k in range(rank)
    ]
    place = lax.broadcasted_iota(jnp.int32, (SUB, width), 0)
    pivots = [jnp.ones((SUB, width), jnp.float32) for _ in range(blocks)]
    for j in range(rank):
        home, spot = divmod(j, SUB)
        column = columns[j]
        pivot = jnp.broadcast_to(column[home][spot : spot + 1], (SUB, width))
        pivots[home] = jnp.where(place == spot, pivot, pivots[home])
        inverse = 1.0 / pivot
        scaled = [None] * blocks
        for b in range(home, blocks):
            scaled[b] = column[b] * inverse
        scaled[home] = jnp.where(place > spot, scaled[home], 0.0)
        for k in range(j + 1, rank):
            other = jnp.broadcast_to(column[k // SUB][k % SUB : k % SUB + 1], (SUB, width))
            for b in range(k // SUB, blocks):
                columns[k][b] = columns[k][b] - scaled[b] * other
        row = jnp.broadcast_to(rows[home][spot : spot + 1], (SUB, width))
        for b in range(home, blocks):
            rows[b] = rows[b] - scaled[b] * row
    return jnp.concatenate([rows[b] * lax.rsqrt(pivots[b]) for b in range(blocks)], axis=0)


def dot(a, b, transposed=False):
    return lax.dot_general(
        a,
        b,
        (((1,), (1 if transposed else 0,)), ((), ())),
        precision=lax.Precision.HIGHEST,
        preferred_element_type=jnp.float32,
    )


def iterate(gram, basis):
    product = dot(basis.T, gram)

    def step(_, product):
        return eliminate(dot(product, product, True), dot(product, gram))

    product = lax.fori_loop(0, ITERS - 1, step, product)
    return eliminate(dot(product, product, True), product)


def basis_kernel(gram_ref, start_ref, basis_ref, narrow_ref):
    basis = iterate(gram_ref[...], start_ref[...])
    basis_ref[...] = basis.T
    narrow_ref[...] = basis.astype(jnp.bfloat16)


def per_device(tensor_field, start_basis):
    fibres = lax.all_to_all(tensor_field, "var", split_axis=1, concat_axis=0, tiled=True)
    partial_gram = jnp.einsum("vc,wc->vw", fibres, fibres, preferred_element_type=jnp.float32)
    gram_matrix = lax.psum(partial_gram, ("space", "var"))
    variables, rank = start_basis.shape
    leading_basis, narrow = pl.pallas_call(
        basis_kernel,
        out_shape=(
            jax.ShapeDtypeStruct((variables, rank), jnp.float32),
            jax.ShapeDtypeStruct((rank, variables), jnp.bfloat16),
        ),
    )(gram_matrix, start_basis)
    core_tensor = jnp.dot(narrow, fibres, preferred_element_type=jnp.float32)
    return (leading_basis, core_tensor)


def solution(mesh):
    return jax.shard_map(
        per_device,
        mesh=mesh,
        in_specs=(P("var", "space"), P()),
        out_specs=(P(), P(None, ("space", "var"))),
        check_vma=False,
    )
```

time: 279 us -> 176 us (0.63)
  other arithmetic: 53.6 us -> 0 us
  waiting for transfers between devices: 163 us -> 117 us
  matrix products: 14.7 us -> 3.44 us
  Pallas kernels: 0 us -> 7.09 us
    another operation x40 -> x0, other arithmetic: 53.5 us -> none  [the longest x24 28.8 us: per_device(): factor = jnp.linalg.cholesky(cross_gram)]
    reduce_scatter x1 -> x0, waiting for transfers between devices: 45.4 us -> none  [per_device(): lax.psum_scatter(core_term, 'var', scatter_dimension=1, tiled=True)]
    dot_general x17 -> x1, matrix products: 11.5 us -> 2.11 us  [per_device(): core_tensor = jnp.dot(narrow, fibres, preferred_element_type=jnp.float32)]
    pallas_call x0 -> x1, Pallas kernels: none -> 7.09 us  [per_device(): pl.pallas_call(basis_kernel, out_shape=(jax.ShapeDtypeStruct((variables,...]
  transfers between devices with their start and end apart: 2 -> 1, of which waited for: 2 -> 1; matrix products, arithmetic and copies ran while one was open for 0% -> 0% of each run, Pallas kernels for 0% -> 0%
where the time goes in v1:
time: 176 us; the launch traced here: 175 us
  waiting for transfers between devices  117 us (66%)
  blocking collectives  29.7 us (17%)
  between operations  14 us (8%)
  Pallas kernels  7.09 us (4%)
  matrix products  3.44 us (2%)
  local copies, waits for them, and re-layouts  3.14 us (2%)
    psum x1, waiting for transfers between devices, per_device(): gram_matrix = lax.psum(partial_gram, ('space', 'var'))  117 us
    all_to_all x1, blocking collectives, per_device(): lax.all_to_all(tensor_field, 'var', split_axis=1, concat_axis=0, tiled=True)  29.7 us
    pallas_call x1, Pallas kernels, per_device(): pl.pallas_call(basis_kernel, out_shape=(jax.ShapeDtypeStruct((variables,...  7.09 us
  transfers between devices with their start and end apart: 1, of which 1 were waited for; matrix products, arithmetic and copies ran while one was open for 0% of the time, Pallas kernels for 0%

profile of v1, /device:TPU:0, one launch (start us, length us, event | category | flops | bytes accessed | tf_op | source)
XLA Modules:
  0.0 174.8 jit_solution(8006987433749936803)
XLA Ops:
  7.2 0.0 all-reduce.2.cloned.1.call-start
  7.2 1.7 copy.16
  8.9 29.7 %all_to_all.19 = bf16[32,4,8192]{2,0,1:T(8,128)(2,1)S(1)} all-to-all(bf16[32,4,8192]{2,0,1:T(8,128)(2,1)S(1)} %bitcast.13), channel_id=1, replica_groups=mesh['space'=8,'var'=4] {'var'}, dimensions={1} | all-to-all | bytes 4194304 | tf_op jit(solution)/shard_map/all_to_all | solution.py:74
  38.7 0.0 copy-start.1
  38.7 1.3 fusion
  40.0 0.0 all-reduce.2.cloned.1.call-update
  40.0 0.0 copy-done.1
  40.1 0.7 copy.12.start_ref
  40.8 117.3 %all-reduce.2.cloned.1.call-done.gram_ref = f32[128,128]{1,0:T(8,128)} async-done(((f32[128,128]{1,0:T(8,128)}), f32[128,128]{1,0:T(8,128)}) %all-reduce.2.cloned.1.call-update) | async-done | bytes 65552 | tf_op jit(solution)/shard_map/psum | solution.py:76
  158.1 7.1 %shard_map.41 = (f32[128,32]{1,0:T(8,128)}, bf16[32,128]{1,0:T(8,128)(2,1)}) custom-call(f32[128,128]{1,0:T(8,128)} %all-reduce.2.cloned.1.call-done.gram_ref, f32[128,32]{1,0:T(8,128)} %copy.12.start_ref), custom_call_target="tpu_custom_call" | custom-call | tf_op jit(solution)/shard_map/pallas_call | solution.py:78
  165.2 0.0 copy-start
  165.2 2.1 %fusion.1 = f32[32,8192]{1,0:T(8,128)} fusion(bf16[32,128]{1,0:T(8,128)(2,1)} %get-tuple-element.5, bf16[128,8192]{1,0:T(8,128)(2,1)S(1)} %bitcast.12), kind=kOutput, calls=%fused_computation.2 | convolution fusion | flops 67108864 | bytes 3153920 | tf_op jit(solution)/shard_map/dot_general | solution.py:85
  167.3 0.0 copy-done
  167.3 0.7 copy.13
Async XLA Ops:
  7.2 150.9 %all-reduce.2.cloned.1.call-start = ((), (), s32[]{:S(2)}) async-start(), calls=%async_computation.1 | async-start | bytes 131072 | tf_op jit(solution)/shard_map/psum | solution.py:76
  38.7 1.4 copy-start.1
  165.2 2.1 %copy-start = (f32[128,32]{1,0:T(8,128)S(1)}, f32[128,32]{1,0:T(8,128)}, u32[]{:S(2)}) copy-start(f32[128,32]{1,0:T(8,128)} %get-tuple-element.12) | copy-start | bytes 49156
Sparse Core Ops, SparseCore 0:
  40.2 117.8 all-reduce.1

commit v2 on v1

--- a/solution.py
+++ b/solution.py
@@ -1,3 +1,5 @@
+import functools
+
 import jax
 import jax.numpy as jnp
 from jax import lax
@@ -7,6 +9,8 @@
 
 ITERS = 8
 SUB = 8
+CHUNKS = 4
+MESH = pl.DeviceIdType.MESH
 
 
 def eliminate(cross_gram, rows):
@@ -64,31 +68,193 @@
     return eliminate(dot(product, product, True), product)
 
 
-def basis_kernel(gram_ref, start_ref, basis_ref, narrow_ref):
-    basis = iterate(gram_ref[...], start_ref[...])
+def kernel(
+    sizes,
+    field_ref,
+    start_ref,
+    basis_ref,
+    core_ref,
+    fibres,
+    core,
+    pieces,
+    landed,
+    slices,
+    whole,
+    own_sem,
+    core_sem,
+    field_send,
+    field_recv,
+    scatter_send,
+    scatter_recv,
+    sum_send,
+    sum_recv,
+    gather_send,
+    gather_recv,
+):
+    n_space, n_var = sizes["space"], sizes["var"]
+    me_space, me_var = lax.axis_index("space"), lax.axis_index("var")
+    slice_rows = field_ref.shape[0]
+    variables, cells = fibres.shape
+    width = cells // CHUNKS
+    height = variables // n_space
+
+    def ahead(axis, distance):
+        return lax.rem(lax.axis_index(axis) + distance, sizes[axis])
+
+    def behind(axis, distance):
+        return lax.rem(lax.axis_index(axis) + sizes[axis] - distance, sizes[axis])
+
+    def rows_of(device):
+        return pl.ds(pl.multiple_of(device * slice_rows, slice_rows), slice_rows)
+
+    def source(device, chunk):
+        start = pl.multiple_of(device * cells + chunk * width, width)
+        return field_ref.at[:, pl.ds(start, width)]
+
+    barrier = pltpu.get_barrier_semaphore()
+    for axis in ("space", "var"):
+        for distance in range(1, sizes[axis]):
+            pl.semaphore_signal(
+                barrier, inc=1, device_id={axis: ahead(axis, distance)}, device_id_type=MESH
+            )
+    pl.semaphore_wait(barrier, n_space + n_var - 2)
+
+    own, sends = [], []
+    for chunk in range(CHUNKS):
+        columns = pl.ds(chunk * width, width)
+        for distance in [n_var // 2] + [d for d in range(1, n_var) if d != n_var // 2]:
+            peer = ahead("var", distance)
+            copy = pltpu.make_async_remote_copy(
+                src_ref=source(peer, chunk),
+                dst_ref=fibres.at[rows_of(me_var), columns],
+                send_sem=field_send.at[chunk, distance],
+                recv_sem=field_recv.at[chunk, distance],
+                device_id={"var": peer},
+                device_id_type=MESH,
+            )
+            copy.start()
+            sends.append(copy)
+        copy = pltpu.make_async_copy(
+            source(me_var, chunk), fibres.at[rows_of(me_var), columns], own_sem.at[chunk]
+        )
+        copy.start()
+        own.append(copy)
+
+    gram = jnp.zeros((variables, variables), jnp.float32)
+    for chunk in range(CHUNKS):
+        columns = pl.ds(chunk * width, width)
+        own[chunk].wait()
+        for distance in range(1, n_var):
+            sender = behind("var", distance)
+            pltpu.make_async_remote_copy(
+                src_ref=source(sender, chunk),
+                dst_ref=fibres.at[rows_of(sender), columns],
+                send_sem=field_send.at[chunk, distance],
+                recv_sem=field_recv.at[chunk, distance],
+                device_id={"var": sender},
+                device_id_type=MESH,
+            ).wait_recv()
+        block = fibres[:, columns]
+        gram = gram + lax.dot_general(
+            block, block, (((1,), (1,)), ((), ())), preferred_element_type=jnp.float32
+        )
+
+    def exchange(axis, source_of, into, send, recv):
+        mine = lax.axis_index(axis)
+        for distance in range(1, sizes[axis]):
+            peer = ahead(axis, distance)
+            copy = pltpu.make_async_remote_copy(
+                src_ref=source_of(peer),
+                dst_ref=into.at[mine],
+                send_sem=send.at[distance],
+                recv_sem=recv.at[distance],
+                device_id={axis: peer},
+                device_id_type=MESH,
+            )
+            copy.start()
+            sends.append(copy)
+        for distance in range(1, sizes[axis]):
+            sender = behind(axis, distance)
+            pltpu.make_async_remote_copy(
+                src_ref=source_of(sender),
+                dst_ref=into.at[sender],
+                send_sem=send.at[distance],
+                recv_sem=recv.at[distance],
+                device_id={axis: sender},
+                device_id_type=MESH,
+            ).wait_recv()
+
+    for s in range(n_space):
+        pieces[s] = gram[s * height : (s + 1) * height]
+    landed[me_space] = pieces[me_space]
+    exchange("space", lambda peer: pieces.at[peer], landed, scatter_send, scatter_recv)
+    slices[me_var] = jnp.sum(landed[...], axis=0)
+    exchange("var", lambda peer: slices.at[me_var], slices, sum_send, sum_recv)
+    whole[me_space] = jnp.sum(slices[...], axis=0)
+    exchange("space", lambda peer: whole.at[me_space], whole, gather_send, gather_recv)
+    gram = whole[...].reshape(variables, variables)
+
+    basis = iterate(gram, start_ref[...])
+    narrow = basis.astype(jnp.bfloat16)
+    stores = []
+    for chunk in range(CHUNKS):
+        columns = pl.ds(chunk * width, width)
+        core[:, columns] = jnp.dot(
+            narrow, fibres[:, columns], preferred_element_type=jnp.float32
+        )
+        copy = pltpu.make_async_copy(
+            core.at[:, columns], core_ref.at[:, columns], core_sem.at[chunk]
+        )
+        copy.start()
+        stores.append(copy)
     basis_ref[...] = basis.T
-    narrow_ref[...] = basis.astype(jnp.bfloat16)
-
-
-def per_device(tensor_field, start_basis):
-    fibres = lax.all_to_all(tensor_field, "var", split_axis=1, concat_axis=0, tiled=True)
-    partial_gram = jnp.einsum("vc,wc->vw", fibres, fibres, preferred_element_type=jnp.float32)
-    gram_matrix = lax.psum(partial_gram, ("space", "var"))
+    for copy in sends:
+        copy.wait_send()
+    for copy in stores:
+        copy.wait()
+
+
+def per_device(sizes, tensor_field, start_basis):
     variables, rank = start_basis.shape
-    leading_basis, narrow = pl.pallas_call(
-        basis_kernel,
+    n_space, n_var = sizes["space"], sizes["var"]
+    cells = tensor_field.shape[1] // n_var
+    height = variables // n_space
+    dma = pltpu.SemaphoreType.DMA
+    return pl.pallas_call(
+        functools.partial(kernel, sizes),
         out_shape=(
             jax.ShapeDtypeStruct((variables, rank), jnp.float32),
-            jax.ShapeDtypeStruct((rank, variables), jnp.bfloat16),
+            jax.ShapeDtypeStruct((rank, cells), jnp.float32),
         ),
-    )(gram_matrix, start_basis)
-    core_tensor = jnp.dot(narrow, fibres, preferred_element_type=jnp.float32)
-    return (leading_basis, core_tensor)
+        in_specs=[pl.BlockSpec(memory_space=pl.ANY), pl.BlockSpec(memory_space=pltpu.VMEM)],
+        out_specs=(pl.BlockSpec(memory_space=pltpu.VMEM), pl.BlockSpec(memory_space=pl.ANY)),
+        scratch_shapes=[
+            pltpu.VMEM((variables, cells), jnp.bfloat16),
+            pltpu.VMEM((rank, cells), jnp.float32),
+            pltpu.VMEM((n_space, height, variables), jnp.float32),
+            pltpu.VMEM((n_space, height, variables), jnp.float32),
+            pltpu.VMEM((n_var, height, variables), jnp.float32),
+            pltpu.VMEM((n_space, height, variables), jnp.float32),
+            dma((CHUNKS,)),
+            dma((CHUNKS,)),
+            dma((CHUNKS, n_var)),
+            dma((CHUNKS, n_var)),
+            dma((n_space,)),
+            dma((n_space,)),
+            dma((n_var,)),
+            dma((n_var,)),
+            dma((n_space,)),
+            dma((n_space,)),
+        ],
+        compiler_params=pltpu.CompilerParams(
+            collective_id=0, has_side_effects=True, vmem_limit_bytes=48 * 2**20
+        ),
+    )(tensor_field, start_basis)
 
 
 def solution(mesh):
     return jax.shard_map(
-        per_device,
+        functools.partial(per_device, dict(mesh.shape)),
         mesh=mesh,
         in_specs=(P("var", "space"), P()),
         out_specs=(P(), P(None, ("space", "var"))),

time: 176 us -> 52.7 us (0.30)
  waiting for transfers between devices: 117 us -> 0 us
  Pallas kernels: 7.09 us -> 47.8 us
  blocking collectives: 29.7 us -> 0 us
  between operations: 14 us -> 0.65 us
  matrix products: 3.44 us -> 0 us
    psum x1 -> x0, waiting for transfers between devices: 117 us -> none  [per_device(): gram_matrix = lax.psum(partial_gram, ('space', 'var'))]
    pallas_call x1, Pallas kernels: 7.09 us -> 47.8 us  [per_device(): pl.pallas_call(functools.partial(kernel, sizes), out_shape=(jax.ShapeDtyp...]
    all_to_all x1 -> x0, blocking collectives: 29.7 us -> none  [per_device(): lax.all_to_all(tensor_field, 'var', split_axis=1, concat_axis=0, tiled=True)]
    dot_general x2 -> x0, matrix products: 3.44 us -> none  [the longest x1 2.11 us: per_device(): core_tensor = jnp.dot(narrow, fibres, preferred_element_type=jnp.float32)]
    unnamed x6 -> x4, local copies, waits for them, and re-layouts: 1.41 us -> 3.37 us
  transfers between devices with their start and end apart: 1 -> 0, of which waited for: 1 -> 0; matrix products, arithmetic and copies ran while one was open for 0% -> 0% of each run, Pallas kernels for 0% -> 0%
where the time goes in v2:
time: 52.7 us; the launch traced here: 52.5 us
  Pallas kernels  47.8 us (91%)
  local copies, waits for them, and re-layouts  4.05 us (8%)
  between operations  0.65 us (1%)
    pallas_call x1, Pallas kernels, per_device(): pl.pallas_call(functools.partial(kernel, sizes), out_shape=(jax.ShapeDtyp...  47.8 us
    unnamed x4, local copies, waits for them, and re-layouts  3.37 us

profile of v2, /device:TPU:0, one launch (start us, length us, event | category | flops | bytes accessed | tf_op | source)
XLA Modules:
  0.0 52.5 jit_solution(17638757098865050820)
XLA Ops:
  0.6 0.8 %copy.4.start_ref = f32[128,32]{1,0:T(8,128)S(1)} copy(f32[128,32]{0,1:T(8,128)} %param.3) | data formatting | bytes 32768 | tf_op args[1]
  1.4 0.0 copy-start
  1.5 1.6 %copy-done = bf16[32,32768]{1,0:T(8,128)(2,1)S(1)} copy-done((bf16[32,32768]{1,0:T(8,128)(2,1)S(1)}, bf16[32,32768]{1,0:T(8,128)(2,1)}, u32[]{:S(2)}) %copy-start) | copy-done | bytes 2097176
  3.0 47.8 %shard_map.41 = (f32[128,32]{1,0:T(8,128)S(1)}, f32[32,8192]{1,0:T(8,128)S(1)}) custom-call(bf16[32,32768]{1,0:T(8,128)(2,1)S(1)} %copy-done, f32[128,32]{1,0:T(8,128)S(1)} %copy.4.start_ref), custom_call_target="tpu_custom_call" | custom-call | tf_op jit(solution)/shard_map/pallas_call | solution.py:223
  50.8 0.7 %copy.5 = f32[128,32]{0,1:T(8,128)} copy(f32[128,32]{1,0:T(8,128)S(1)} %get-tuple-element.2) | data formatting | bytes 32768 | tf_op jit(solution)/shard_map/pallas_call | solution.py:223
  51.5 1.0 %copy.7 = f32[32,8192]{1,0:T(8,128)} copy(f32[32,8192]{1,0:T(8,128)S(1)} %get-tuple-element.7) | data formatting | bytes 2097152
Async XLA Ops:
  1.4 1.6 %copy-start = (bf16[32,32768]{1,0:T(8,128)(2,1)S(1)}, bf16[32,32768]{1,0:T(8,128)(2,1)}, u32[]{:S(2)}) copy-start(bf16[32,32768]{1,0:T(8,128)(2,1)} %field_ref.1) | copy-start | bytes 6291460

commit v3 on v2

--- a/solution.py
+++ b/solution.py
@@ -48,40 +48,53 @@
     return jnp.concatenate([rows[b] * lax.rsqrt(pivots[b]) for b in range(blocks)], axis=0)
 
 
-def dot(a, b, transposed=False):
+def split(value):
+    high = value.astype(jnp.bfloat16)
+    rest = value - high.astype(jnp.float32)
+    middle = rest.astype(jnp.bfloat16)
+    return high, middle, (rest - middle.astype(jnp.float32)).astype(jnp.bfloat16)
+
+
+def join(terms, order, axis):
+    return jnp.concatenate([terms[i] for i in order], axis=axis)
+
+
+LEFT, RIGHT = (1, 0, 2, 0, 1, 0), (1, 2, 0, 1, 0, 0)
+
+
+def dot(a, b, axis):
     return lax.dot_general(
-        a,
-        b,
-        (((1,), (1 if transposed else 0,)), ((), ())),
-        precision=lax.Precision.HIGHEST,
-        preferred_element_type=jnp.float32,
+        a, b, (((1,), (axis,)), ((), ())), preferred_element_type=jnp.float32
     )
 
 
-def iterate(gram, basis):
-    product = dot(basis.T, gram)
+def iterate(gram, basis, split_gram):
+    split_gram[...] = join(split(gram), RIGHT, 0)
+    product = dot(join(split(basis), LEFT, 1), split_gram[...], 0)
 
     def step(_, product):
-        return eliminate(dot(product, product, True), dot(product, gram))
+        terms = split(product)
+        left = join(terms, LEFT, 1)
+        cross_gram = dot(left, join(terms, RIGHT, 1), 1)
+        return eliminate(cross_gram, dot(left, split_gram[...], 0))
 
     product = lax.fori_loop(0, ITERS - 1, step, product)
-    return eliminate(dot(product, product, True), product)
-
-
-def kernel(
+    terms = split(product)
+    return eliminate(dot(join(terms, LEFT, 1), join(terms, RIGHT, 1), 1), product)
+
+
+def gram_kernel(
     sizes,
     field_ref,
-    start_ref,
-    basis_ref,
-    core_ref,
+    gram_ref,
+    fibres_ref,
     fibres,
-    core,
     pieces,
     landed,
     slices,
     whole,
+    keep_sem,
     own_sem,
-    core_sem,
     field_send,
     field_recv,
     scatter_send,
@@ -96,7 +109,7 @@
     slice_rows = field_ref.shape[0]
     variables, cells = fibres.shape
     width = cells // CHUNKS
-    height = variables // n_space
+    height = variables // n_var
 
     def ahead(axis, distance):
         return lax.rem(lax.axis_index(axis) + distance, sizes[axis])
@@ -158,6 +171,9 @@
         gram = gram + lax.dot_general(
             block, block, (((1,), (1,)), ((), ())), preferred_element_type=jnp.float32
         )
+
+    keep = pltpu.make_async_copy(fibres, fibres_ref, keep_sem)
+    keep.start()
 
     def exchange(axis, source_of, into, send, recv):
         mine = lax.axis_index(axis)
@@ -184,18 +200,30 @@
                 device_id_type=MESH,
             ).wait_recv()
 
-    for s in range(n_space):
-        pieces[s] = gram[s * height : (s + 1) * height]
-    landed[me_space] = pieces[me_space]
-    exchange("space", lambda peer: pieces.at[peer], landed, scatter_send, scatter_recv)
-    slices[me_var] = jnp.sum(landed[...], axis=0)
-    exchange("var", lambda peer: slices.at[me_var], slices, sum_send, sum_recv)
-    whole[me_space] = jnp.sum(slices[...], axis=0)
-    exchange("space", lambda peer: whole.at[me_space], whole, gather_send, gather_recv)
-    gram = whole[...].reshape(variables, variables)
-
-    basis = iterate(gram, start_ref[...])
+    for v in range(n_var):
+        pieces[v] = gram[v * height : (v + 1) * height]
+    landed[me_var] = pieces[me_var]
+    exchange("var", lambda peer: pieces.at[peer], landed, scatter_send, scatter_recv)
+    slices[me_space] = jnp.sum(landed[...], axis=0)
+    exchange("space", lambda peer: slices.at[me_space], slices, sum_send, sum_recv)
+    whole[me_var] = jnp.sum(slices[...], axis=0)
+    exchange("var", lambda peer: whole.at[me_var], whole, gather_send, gather_recv)
+    gram_ref[...] = whole[...].reshape(variables, variables)
+    for copy in sends:
+        copy.wait_send()
+    keep.wait()
+
+
+def core_kernel(
+    gram_ref, start_ref, fibres_ref, basis_ref, core_ref, fibres, core, split_gram, load_sem, core_sem
+):
+    load = pltpu.make_async_copy(fibres_ref, fibres, load_sem)
+    load.start()
+    basis = iterate(gram_ref[...], start_ref[...], split_gram)
+    basis_ref[...] = basis
     narrow = basis.astype(jnp.bfloat16)
+    load.wait()
+    width = fibres.shape[1] // CHUNKS
     stores = []
     for chunk in range(CHUNKS):
         columns = pl.ds(chunk * width, width)
@@ -207,9 +235,6 @@
         )
         copy.start()
         stores.append(copy)
-    basis_ref[...] = basis.T
-    for copy in sends:
-        copy.wait_send()
     for copy in stores:
         copy.wait()
 
@@ -218,38 +243,56 @@
     variables, rank = start_basis.shape
     n_space, n_var = sizes["space"], sizes["var"]
     cells = tensor_field.shape[1] // n_var
-    height = variables // n_space
+    height = variables // n_var
     dma = pltpu.SemaphoreType.DMA
-    return pl.pallas_call(
-        functools.partial(kernel, sizes),
+    in_vmem, anywhere = pl.BlockSpec(memory_space=pltpu.VMEM), pl.BlockSpec(memory_space=pl.ANY)
+    gram, fibres = pl.pallas_call(
+        functools.partial(gram_kernel, sizes),
         out_shape=(
-            jax.ShapeDtypeStruct((variables, rank), jnp.float32),
-            jax.ShapeDtypeStruct((rank, cells), jnp.float32),
+            jax.ShapeDtypeStruct((variables, variables), jnp.float32),
+            jax.ShapeDtypeStruct((variables, cells), jnp.bfloat16),
         ),
-        in_specs=[pl.BlockSpec(memory_space=pl.ANY), pl.BlockSpec(memory_space=pltpu.VMEM)],
-        out_specs=(pl.BlockSpec(memory_space=pltpu.VMEM), pl.BlockSpec(memory_space=pl.ANY)),
+        in_specs=[anywhere],
+        out_specs=(in_vmem, anywhere),
         scratch_shapes=[
             pltpu.VMEM((variables, cells), jnp.bfloat16),
-            pltpu.VMEM((rank, cells), jnp.float32),
-            pltpu.VMEM((n_space, height, variables), jnp.float32),
+            pltpu.VMEM((n_var, height, variables), jnp.float32),
+            pltpu.VMEM((n_var, height, variables), jnp.float32),
             pltpu.VMEM((n_space, height, variables), jnp.float32),
             pltpu.VMEM((n_var, height, variables), jnp.float32),
-            pltpu.VMEM((n_space, height, variables), jnp.float32),
-            dma((CHUNKS,)),
+            dma(()),
             dma((CHUNKS,)),
             dma((CHUNKS, n_var)),
             dma((CHUNKS, n_var)),
+            dma((n_var,)),
+            dma((n_var,)),
             dma((n_space,)),
             dma((n_space,)),
             dma((n_var,)),
             dma((n_var,)),
-            dma((n_space,)),
-            dma((n_space,)),
         ],
         compiler_params=pltpu.CompilerParams(
-            collective_id=0, has_side_effects=True, vmem_limit_bytes=48 * 2**20
+            collective_id=0, has_side_effects=True, vmem_limit_bytes=60 * 2**20
         ),
-    )(tensor_field, start_basis)
+    )(tensor_field)
+    basis, core = pl.pallas_call(
+        core_kernel,
+        out_shape=(
+            jax.ShapeDtypeStruct((rank, variables), jnp.float32),
+            jax.ShapeDtypeStruct((rank, cells), jnp.float32),
+        ),
+        in_specs=[in_vmem, in_vmem, anywhere],
+        out_specs=(in_vmem, anywhere),
+        scratch_shapes=[
+            pltpu.VMEM((variables, cells), jnp.bfloat16),
+            pltpu.VMEM((rank, cells), jnp.float32),
+            pltpu.VMEM((len(RIGHT) * variables, variables), jnp.bfloat16),
+            dma(()),
+            dma((CHUNKS,)),
+        ],
+        compiler_params=pltpu.CompilerParams(vmem_limit_bytes=60 * 2**20),
+    )(gram, start_basis.T, fibres)
+    return basis.T, core
 
 
 def solution(mesh):

time: 52.7 us -> 49.3 us (0.935)
  local copies, waits for them, and re-layouts: 4.05 us -> 0 us
  Pallas kernels: 47.8 us -> 48.5 us
    unnamed x4 -> x0, local copies, waits for them, and re-layouts: 3.37 us -> none
    pallas_call x1 -> x2, Pallas kernels: 47.8 us -> 48.5 us  [the longest x1 40.4 us: per_device(): pl.pallas_call(functools.partial(gram_kernel, sizes), out_shape=(jax.Shap...]
    pallas_call x1 -> x0, local copies, waits for them, and re-layouts: 0.68 us -> none  [per_device(): pl.pallas_call(functools.partial(kernel, sizes), out_shape=(jax.ShapeDtyp...]
where the time goes in v3:
time: 49.3 us; the launch traced here: 49.1 us
  Pallas kernels  48.5 us (98%)
  between operations  0.64 us (1%)
    pallas_call x1, Pallas kernels, per_device(): pl.pallas_call(functools.partial(gram_kernel, sizes), out_shape=(jax.Shap...  40.4 us
    pallas_call x1, Pallas kernels, per_device(): pl.pallas_call(core_kernel, out_shape=(jax.ShapeDtypeStruct((rank, variab...  8.05 us

profile of v3, /device:TPU:0, one launch (start us, length us, event | category | flops | bytes accessed | tf_op | source)
XLA Modules:
  0.0 49.1 jit_solution(5305578160303087095)
XLA Ops:
  0.6 40.4 %shard_map.41 = (f32[128,128]{1,0:T(8,128)}, bf16[128,8192]{1,0:T(8,128)(2,1)}) custom-call(bf16[32,32768]{1,0:T(8,128)(2,1)} %field_ref.1), custom_call_target="tpu_custom_call" | custom-call | tf_op jit(solution)/shard_map/pallas_call | solution.py:249
  41.1 8.1 %shard_map.42 = (f32[32,128]{1,0:T(8,128)}, f32[32,8192]{1,0:T(8,128)}) custom-call(f32[128,128]{1,0:T(8,128)} %get-tuple-element.6.gram_ref, f32[32,128]{1,0:T(8,128)} %bitcast.2, bf16[128,8192]{1,0:T(8,128)(2,1)} %get-tuple-element.7.fibres_ref), custom_call_target="tpu_custom_call" | custom-call | tf_op jit(solution)/shard_map/pallas_call | solution.py:278
